TPU v7x, 32 devices: a whole 2x2x4 slice. The times are simulated.
32 devices in a mesh: groups: 2 (over x), band: 2 (over core), gz: 8 (over z, y).
Axes of the slice: x: 2, y: 2, z: 4, core: 2. Of those that a mesh axis runs over, the one named last changes fastest.
Arguments:
- orbitals: bfloat16 [24, 64, 256, 256], P(('groups', 'band'), 'gz'), parts along dimension 0, may hold values from -3 to 3
- band_group: int32 [24], P(('groups', 'band')), parts along dimension 0, may hold values from 0 to 7
- occ_table: int32 [8], replicated, may hold values from 0 to 2048
- core_density: float32 [128, 256, 256], P(('groups', 'gz')), parts along dimension 0, may hold values from 0.1 to 12
Outputs:
- potential: float32 [128, 256, 256], P(('groups', 'gz')), parts along dimension 0
- residual: float32 [128, 256, 256], P(('groups', 'gz'), 'band'), parts along dimension 0
There are 2 independent parts, one for each index of `groups`. A program takes and returns all parts, laid end to end along the dimension named above; an argument that names none is the same for every part. Nothing has to cross between parts.
All inputs are finite; a program needn't handle non-finite values.
Results may differ from a plain program's by a relative error of at most 0.0003.
Values sent between devices are 32-bit elements; how exact they have to be, the bound alone decides.
A program may use at most 64 MiB of HBM per device.

v0:
```python
import math

import jax
import jax.numpy as jnp
from jax import lax
from jax.sharding import PartitionSpec as P

ITERS = 3


solvent_eps = 78.36
density_low = 2.0
density_high = 12.0
screening = 0.05
coupling = 1.0 / (4.0 * math.pi)


def extended(shard, sides, width):
    for axis, dim in sides:
        size, length = (lax.axis_size(axis), shard.shape[dim])
        up = [(i, (i + 1) % size) for i in range(size)]
        down = [(j, i) for i, j in up]
        last = lax.slice_in_dim(shard, length - width, length, axis=dim)
        initial = lax.slice_in_dim(shard, 0, width, axis=dim)
        before = lax.ppermute(last, axis, up)
        after = lax.ppermute(initial, axis, down)
        shard = jnp.concatenate([before, shard, after], axis=dim)
    return shard


def band_weights(band_group, occ_table):
    levels = occ_table.shape[0]
    matches = band_group[:, None] == jnp.arange(levels, dtype=jnp.int32)[None, :]
    chosen = jnp.where(matches, occ_table[None, :], 0)
    return jnp.sum(chosen, axis=1).astype(jnp.float32) / 1024.0


def dielectric(density):
    span = math.log(density_high) - math.log(density_low)
    fraction = jnp.clip((math.log(density_high) - jnp.log(density)) / span, 0.0, 1.0)
    turned = 2.0 * math.pi * fraction
    return jnp.exp(math.log(solvent_eps) / (2.0 * math.pi) * (turned - jnp.sin(turned)))


def extend(values):
    padded = extended(values, (("band", 1), ("gz", 0)), 1)
    return padded


def face_coefs(eps):
    padded = extend(eps)
    center = padded[1:-1, 1:-1]
    half = 0.5 * coupling
    return (
        half * (center + padded[:-2, 1:-1]),
        half * (center + padded[2:, 1:-1]),
        half * (center + padded[1:-1, :-2]),
        half * (center + padded[1:-1, 2:]),
        half * (center + jnp.roll(center, 1, 2)),
        half * (center + jnp.roll(center, -1, 2)),
    )


def operate(values, coefs, diagonal):
    padded = extend(values)
    center = padded[1:-1, 1:-1]
    result = diagonal * center
    result = result - coefs[0] * padded[:-2, 1:-1] - coefs[1] * padded[2:, 1:-1]
    result = result - coefs[2] * padded[1:-1, :-2] - coefs[3] * padded[1:-1, 2:]
    result = result - coefs[4] * jnp.roll(center, 1, 2) - coefs[5] * jnp.roll(center, -1, 2)
    return result


def reduce_one(value):
    summed = lax.psum(value, ("band", "gz"))
    return summed


def solve(source, coefs, diagonal):
    potential = jnp.zeros_like(source)
    residual = source
    precond = residual / diagonal
    direction = precond
    inner_now = reduce_one(jnp.sum(residual * precond))
    for step in range(ITERS):
        image = operate(direction, coefs, diagonal)
        step_size = inner_now / reduce_one(jnp.sum(direction * image))
        potential = potential + step_size * direction
        residual = residual - step_size * image
        if step + 1 < ITERS:
            precond = residual / diagonal
            inner_next = reduce_one(jnp.sum(residual * precond))
            direction = precond + inner_next / inner_now * direction
            inner_now = inner_next
    return (potential, residual)


def per_device(orbitals, band_group, occ_table, core_density):
    weights = band_weights(band_group, occ_table)
    squares = jnp.square(orbitals.astype(jnp.float32))
    partial_value = jnp.sum(weights[:, None, None, None] * squares, axis=0)
    electrons = lax.psum_scatter(partial_value, "band", scatter_dimension=1, tiled=True)
    width = electrons.shape[1]
    core = lax.dynamic_slice_in_dim(core_density, lax.axis_index("band") * width, width, 1)
    density = electrons + core
    source = electrons - core
    eps = dielectric(density)
    coefs = face_coefs(eps)
    diagonal = screening + coefs[0] + coefs[1] + coefs[2] + coefs[3] + coefs[4] + coefs[5]
    solution, residual = solve(source, coefs, diagonal)
    potential = lax.all_gather(solution, "band", axis=1, tiled=True)
    return (potential, residual)


def solution(mesh):
    return jax.shard_map(
        per_device,
        mesh=mesh,
        in_specs=(
            P(("groups", "band"), "gz", None, None),
            P(("groups", "band")),
            P(),
            P(("groups", "gz"), None, None),
        ),
        out_specs=(P(("groups", "gz"), None, None), P(("groups", "gz"), "band", None)),
        check_vma=False,
    )
```

profile of v0, /device:TPU:0, one launch (start us, length us, event | category | flops | bytes accessed | tf_op | source)
XLA Modules:
  0.0 291.4 jit_solution(6546125435858328267)
XLA Ops:
  8.1 6.0 %multiply_reduce_fusion = f32[8,256,256]{2,1,0:T(8,128)} fusion(bf16[6,8,256,256]{3,2,1,0:T(8,128)(2,1)} %param.4, f32[6]{0:T(128)S(1)} %convert_multiply_fusion), kind=kLoop, calls=%fused_computation | loop fusion | flops 12058624 | bytes 8388632 | tf_op jit(solution)/shard_map/reduce_sum | solution.py:101
  14.2 12.4 %reduce-scatter.2.cloned.1.call-done = f32[8,128,256]{2,1,0:T(8,128)} async-done(((f32[8,256,256]{2,1,0:T(8,128)}), f32[8,128,256]{2,1,0:T(8,128)}) %reduce-scatter.2.cloned.1.call-update) | async-done | bytes 1048592 | tf_op jit(solution)/shard_map/reduce_scatter | solution.py:102
  26.6 4.8 %fusion.1 = f32[8,128,256]{2,1,0:T(8,128)S(1)} fusion(f32[8,128,256]{2,1,0:T(8,128)} %reduce-scatter.2.cloned.1.call-done, f32[8,256,256]{2,1,0:T(8,128)S(1)} %copy-done.19, s32[]{:T(128)S(6)} %select_n.8), kind=kLoop, calls=%fused_computation.3 | loop fusion | flops 1835008 | bytes 3145732 | tf_op jit(solution)/shard_map/exp | solution.py:42
  32.9 1.9 collective-permute-start.2
  34.8 2.9 collective-permute-start.3
  37.9 3.8 %collective-permute-done.2 = f32[1,130,256]{2,1,0:T(8,128)S(1)} collective-permute-done((f32[1,130,256]{2,1,0:T(8,128)S(1)}, f32[1,130,256]{2,1,0:T(8,128)S(1)}, u32[]{:S(2)}, u32[]{:S(2)}) %collective-permute-start.2) | collective-permute-done | bytes 133152 | tf_op jit(solution)/shard_map/ppermute | solution.py:25
  41.7 1.6 collective-permute-done.3
  43.3 2.0 fusion.45
  47.1 4.4 %collective-permute-start.7 = (f32[1,130,256]{2,1,0:T(8,128)S(1)}, f32[1,130,256]{2,1,0:T(8,128)S(1)}, u32[]{:S(2)}, u32[]{:S(2)}) collective-permute-start(f32[1,130,256]{2,1,0:T(8,128)S(1)} %get-tuple-element.25), channel_id=1, source_target_pairs={{1,0},{2,1},{3,2},{4,3},{5,4},{6,5},{7,6},{0,7},{9,8},{10,9},{11,1... | collective-permute-start | bytes 399368 | tf_op jit(solution)/shard_map/ppermute | solution.py:26
  51.7 3.8 %collective-permute-done.6 = f32[1,130,256]{2,1,0:T(8,128)S(1)} collective-permute-done((f32[1,130,256]{2,1,0:T(8,128)S(1)}, f32[1,130,256]{2,1,0:T(8,128)S(1)}, u32[]{:S(2)}, u32[]{:S(2)}) %collective-permute-start.6) | collective-permute-done | bytes 133152 | tf_op jit(solution)/shard_map/ppermute | solution.py:25
  56.4 5.0 %multiply_reduce_fusion.5 = (f32[]{:T(128)}, f32[]{:T(128)}, f32[8,128,256]{2,1,0:T(8,128)}) fusion(f32[8,128,256]{2,1,0:T(8,128)S(1)} %get-tuple-element.17, f32[8,128,256]{2,1,0:T(8,128)S(1)} %get-tuple-element.19, f32[8,128,1]{2,1,0:T(8,128)S(1)} %get-tuple-element.43, f32[8,128,255]{2,1,0:T(8,128)S(1)} %get-tuple-element.45, ...), kind=kLoop, calls=%fused_computation.94 | loop fusion | flops 12845054 | bytes 10002440 | tf_op jit(solution)/shard_map/reduce_sum | solution.py:87
  61.4 32.5 %all-reduce = (f32[]{:T(128)}, f32[]{:T(128)}) all-reduce(f32[]{:T(128)} %get-tuple-element.3, f32[]{:T(128)} %get-tuple-element.2), channel_id=1, replica_groups=mesh['groups'=2,'band'=2,'gz'=8] {'band','gz'}, use_global_device_ids=true, to_apply=%region_4.5 | all-reduce | flops 2 | bytes 16 | tf_op jit(solution)/shard_map/psum | solution.py:75
  95.1 3.8 %multiply_reduce_fusion.4 = (f32[]{:T(128)}, f32[8,128,256]{2,1,0:T(8,128)}, f32[8,128,256]{2,1,0:T(8,128)}) fusion(f32[8,128,256]{2,1,0:T(8,128)S(1)} %get-tuple-element.18, f32[8,128,256]{2,1,0:T(8,128)} %copy-done.16, f32[8,128,256]{2,1,0:T(8,128)} %get-tuple-element.16, f32[]{:T(128)S(6)} %div.37), kind=kLoop, calls=%fused_computation.92 | loop fusion | flops 1310719 | bytes 5242888 | tf_op jit(solution)/shard_map/reduce_sum | solution.py:92
  98.9 30.2 %psum.44 = f32[]{:T(128)} all-reduce(f32[]{:T(128)} %get-tuple-element.13), channel_id=1, replica_groups=mesh['groups'=2,'band'=2,'gz'=8] {'band','gz'}, use_global_device_ids=true, to_apply=%region_8.9 | all-reduce | flops 1 | bytes 8 | tf_op jit(solution)/shard_map/psum | solution.py:75
  130.3 1.4 multiply_add_fusion.2
  134.3 1.6 collective-permute-start.10
  135.9 3.2 %collective-permute-start.11 = (f32[1,130,256]{2,1,0:T(8,128)S(1)}, f32[1,130,256]{2,1,0:T(8,128)S(1)}, u32[]{:S(2)}, u32[]{:S(2)}) collective-permute-start(f32[1,130,256]{2,1,0:T(8,128)S(1)} %get-tuple-element.23), channel_id=1, source_target_pairs={{1,0},{2,1},{3,2},{4,3},{5,4},{6,5},{7,6},{0,7},{9,8},{10,9},{11,1... | collective-permute-start | bytes 399368 | tf_op jit(solution)/shard_map/ppermute | solution.py:26
  139.3 3.6 %collective-permute-done.10 = f32[1,130,256]{2,1,0:T(8,128)S(1)} collective-permute-done((f32[1,130,256]{2,1,0:T(8,128)S(1)}, f32[1,130,256]{2,1,0:T(8,128)S(1)}, u32[]{:S(2)}, u32[]{:S(2)}) %collective-permute-start.10) | collective-permute-done | bytes 133152 | tf_op jit(solution)/shard_map/ppermute | solution.py:25
  142.9 1.4 collective-permute-done.11
  144.4 4.8 %multiply_reduce_fusion.3 = (f32[]{:T(128)}, f32[8,128,256]{2,1,0:T(8,128)}) fusion(f32[8,128,256]{2,1,0:T(8,128)S(1)} %multiply_add_fusion.2, f32[8,128,1]{2,1,0:T(8,128)S(1)} %get-tuple-element.37, f32[8,128,255]{2,1,0:T(8,128)S(1)} %get-tuple-element.39, f32[8,128,256]{2,1,0:T(8,128)S(1)} %fusion.1, f32[8,128,1]{2,1,0:T(8,128)S(1)} %copy-done.14, ...), kind=kLoop, calls=%fused_computation.90 | loop fusion | flops 12320767 | bytes 8953860 | tf_op jit(solution)/shard_map/reduce_sum | solution.py:87
  149.1 31.6 %psum.45 = f32[]{:T(128)} all-reduce(f32[]{:T(128)} %get-tuple-element.11), channel_id=1, replica_groups=mesh['groups'=2,'band'=2,'gz'=8] {'band','gz'}, use_global_device_ids=true, to_apply=%region_10.11 | all-reduce | flops 1 | bytes 8 | tf_op jit(solution)/shard_map/psum | solution.py:75
  182.0 4.1 %multiply_reduce_fusion.2 = (f32[]{:T(128)}, f32[8,128,256]{2,1,0:T(8,128)}, f32[8,128,256]{2,1,0:T(8,128)}) fusion(f32[8,128,256]{2,1,0:T(8,128)} %copy-done.1, f32[8,128,256]{2,1,0:T(8,128)} %get-tuple-element.15, f32[8,128,256]{2,1,0:T(8,128)} %get-tuple-element.12, f32[]{:T(128)S(6)} %div.40), kind=kLoop, calls=%fused_computation.88 | loop fusion | flops 1310719 | bytes 5242888 | tf_op jit(solution)/shard_map/reduce_sum | solution.py:92
  186.1 31.1 %psum.46 = f32[]{:T(128)} all-reduce(f32[]{:T(128)} %get-tuple-element.8), channel_id=1, replica_groups=mesh['groups'=2,'band'=2,'gz'=8] {'band','gz'}, use_global_device_ids=true, to_apply=%region_12.13 | all-reduce | flops 1 | bytes 8 | tf_op jit(solution)/shard_map/psum | solution.py:75
  221.9 1.5 collective-permute-start.14
  223.4 3.3 %collective-permute-start.15 = (f32[1,130,256]{2,1,0:T(8,128)S(1)}, f32[1,130,256]{2,1,0:T(8,128)S(1)}, u32[]{:S(2)}, u32[]{:S(2)}) collective-permute-start(f32[1,130,256]{2,1,0:T(8,128)S(1)} %get-tuple-element.21), channel_id=1, source_target_pairs={{1,0},{2,1},{3,2},{4,3},{5,4},{6,5},{7,6},{0,7},{9,8},{10,9},{11,1... | collective-permute-start | bytes 399368 | tf_op jit(solution)/shard_map/ppermute | solution.py:26
  226.9 3.6 %collective-permute-done.14 = f32[1,130,256]{2,1,0:T(8,128)S(1)} collective-permute-done((f32[1,130,256]{2,1,0:T(8,128)S(1)}, f32[1,130,256]{2,1,0:T(8,128)S(1)}, u32[]{:S(2)}, u32[]{:S(2)}) %collective-permute-start.14) | collective-permute-done | bytes 133152 | tf_op jit(solution)/shard_map/ppermute | solution.py:25
  231.9 4.8 %multiply_reduce_fusion.1 = (f32[]{:T(128)}, f32[8,128,256]{2,1,0:T(8,128)}) fusion(f32[8,128,256]{2,1,0:T(8,128)S(1)} %multiply_add_fusion.1, f32[8,128,1]{2,1,0:T(8,128)S(1)} %get-tuple-element.31, f32[8,128,255]{2,1,0:T(8,128)S(1)} %get-tuple-element.33, f32[8,128,256]{2,1,0:T(8,128)S(1)} %fusion.1, f32[8,128,1]{2,1,0:T(8,128)S(1)} %copy-done.15, ...), kind=kLoop, calls=%fused_computation.86 | loop fusion | flops 12320767 | bytes 8953860 | tf_op jit(solution)/shard_map/reduce_sum | solution.py:87
  236.7 31.8 %psum.47 = f32[]{:T(128)} all-reduce(f32[]{:T(128)} %get-tuple-element.6), channel_id=1, replica_groups=mesh['groups'=2,'band'=2,'gz'=8] {'band','gz'}, use_global_device_ids=true, to_apply=%region_14.15 | all-reduce | flops 1 | bytes 8 | tf_op jit(solution)/shard_map/psum | solution.py:75
  269.8 2.5 multiply_add_fusion
  272.4 2.3 multiply_subtract_fusion
  274.7 6.8 %all-gather.2.cloned.1.call-done = f32[8,256,256]{2,1,0:T(8,128)} async-done(((f32[8,128,256]{2,1,0:T(8,128)}), f32[8,256,256]{2,1,0:T(8,128)}) %all-gather.2.cloned.1.call-update) | async-done | bytes 2097168 | tf_op jit(solution)/shard_map/all_gather | solution.py:111
  281.5 3.0 %copy.7 = f32[8,256,256]{2,1,0:T(8,128)} copy(f32[8,256,256]{2,1,0:T(8,128)} %all-gather.2.cloned.1.call-done) | data formatting | bytes 4194304
  (84 shorter events, 13.1 us)
Async XLA Ops:
  7.2 19.4 %reduce-scatter.2.cloned.1.call-start = ((), (), s32[]{:S(2)}) async-start(), calls=%async_computation.1 | async-start | bytes 3145728 | tf_op jit(solution)/shard_map/reduce_scatter | solution.py:102
  14.1 12.5 %copy-start.19 = (f32[8,256,256]{2,1,0:T(8,128)S(1)}, f32[8,256,256]{2,1,0:T(8,128)}, u32[]{:S(2)}) copy-start(f32[8,256,256]{2,1,0:T(8,128)} %param.7) | copy-start | bytes 6291460
  14.1 267.3 %all-gather.2.cloned.1.call-start = ((), (), s32[]{:S(2)}) async-start(), calls=%async_computation.2 | async-start | bytes 3145728 | tf_op jit(solution)/shard_map/all_gather | solution.py:111
  31.4 1.2 collective-permute-start
  31.7 1.2 collective-permute-start.1
  32.4 24.0 %copy-start.4 = (f32[8,128,255]{2,1,0:T(8,128)}, f32[8,128,255]{2,1,0:T(8,128)S(1)}, u32[]{:S(2)}) copy-start(f32[8,128,255]{2,1,0:T(8,128)S(1)} %get-tuple-element.50) | copy-start | bytes 3133444
  32.4 24.0 %copy-start.7 = (f32[8,128,255]{2,1,0:T(8,128)}, f32[8,128,255]{2,1,0:T(8,128)S(1)}, u32[]{:S(2)}) copy-start(f32[8,128,255]{2,1,0:T(8,128)S(1)} %get-tuple-element.51) | copy-start | bytes 3133444
  32.4 10.9 %copy-start.17 = (f32[8,128,256]{2,1,0:T(8,128)S(1)}, f32[8,128,256]{2,1,0:T(8,128)}, u32[]{:S(2)}) copy-start(f32[8,128,256]{2,1,0:T(8,128)} %reduce-scatter.2.cloned.1.call-done) | copy-start | bytes 3145732
  32.4 10.9 %copy-start.20 = (f32[8,256,256]{2,1,0:T(8,128)S(1)}, f32[8,256,256]{2,1,0:T(8,128)}, u32[]{:S(2)}) copy-start(f32[8,256,256]{2,1,0:T(8,128)} %param.7) | copy-start | bytes 6291460
  32.9 8.8 %collective-permute-start.2 = (f32[1,130,256]{2,1,0:T(8,128)S(1)}, f32[1,130,256]{2,1,0:T(8,128)S(1)}, u32[]{:S(2)}, u32[]{:S(2)}) collective-permute-start(f32[1,130,256]{2,1,0:T(8,128)S(1)} %get-tuple-element.26), channel_id=1, source_target_pairs={{0,1},{1,2},{2,3},{3,4},{4,5},{5,6},{6,7},{7,0},{8,9},{9,10},{10,1... | collective-permute-start | bytes 399368 | tf_op jit(solution)/shard_map/ppermute | solution.py:25
  34.8 8.5 %collective-permute-start.3 = (f32[1,130,256]{2,1,0:T(8,128)S(1)}, f32[1,130,256]{2,1,0:T(8,128)S(1)}, u32[]{:S(2)}, u32[]{:S(2)}) collective-permute-start(f32[1,130,256]{2,1,0:T(8,128)S(1)} %get-tuple-element.27), channel_id=1, source_target_pairs={{1,0},{2,1},{3,2},{4,3},{5,4},{6,5},{7,6},{0,7},{9,8},{10,9},{11,1... | collective-permute-start | bytes 399368 | tf_op jit(solution)/shard_map/ppermute | solution.py:26
  37.9 18.5 %copy-start.10 = (f32[8,128,1]{2,1,0:T(8,128)}, f32[8,128,1]{2,1,0:T(8,128)S(1)}, u32[]{:S(2)}) copy-start(f32[8,128,1]{2,1,0:T(8,128)S(1)} %get-tuple-element.48) | copy-start | bytes 12292
  37.9 18.5 %copy-start.13 = (f32[8,128,1]{2,1,0:T(8,128)}, f32[8,128,1]{2,1,0:T(8,128)S(1)}, u32[]{:S(2)}) copy-start(f32[8,128,1]{2,1,0:T(8,128)S(1)} %get-tuple-element.49) | copy-start | bytes 12292
  45.3 11.1 %copy-start.16 = (f32[8,128,256]{2,1,0:T(8,128)}, f32[8,128,256]{2,1,0:T(8,128)S(1)}, u32[]{:S(2)}) copy-start(f32[8,128,256]{2,1,0:T(8,128)S(1)} %get-tuple-element.19) | copy-start | bytes 3145732
  45.3 49.8 %copy-start.1 = (f32[8,128,256]{2,1,0:T(8,128)}, f32[8,128,256]{2,1,0:T(8,128)S(1)}, u32[]{:S(2)}) copy-start(f32[8,128,256]{2,1,0:T(8,128)S(1)} %get-tuple-element.18) | copy-start | bytes 3145732
  45.3 1.2 collective-permute-start.4
  45.4 1.3 collective-permute-start.5
  46.7 8.8 %collective-permute-start.6 = (f32[1,130,256]{2,1,0:T(8,128)S(1)}, f32[1,130,256]{2,1,0:T(8,128)S(1)}, u32[]{:S(2)}, u32[]{:S(2)}) collective-permute-start(f32[1,130,256]{2,1,0:T(8,128)S(1)} %get-tuple-element.24), channel_id=1, source_target_pairs={{0,1},{1,2},{2,3},{3,4},{4,5},{5,6},{6,7},{7,0},{8,9},{9,10},{10,1... | collective-permute-start | bytes 399368 | tf_op jit(solution)/shard_map/ppermute | solution.py:25
  47.1 9.2 %collective-permute-start.7 = (f32[1,130,256]{2,1,0:T(8,128)S(1)}, f32[1,130,256]{2,1,0:T(8,128)S(1)}, u32[]{:S(2)}, u32[]{:S(2)}) collective-permute-start(f32[1,130,256]{2,1,0:T(8,128)S(1)} %get-tuple-element.25), channel_id=1, source_target_pairs={{1,0},{2,1},{3,2},{4,3},{5,4},{6,5},{7,6},{0,7},{9,8},{10,9},{11,1... | collective-permute-start | bytes 399368 | tf_op jit(solution)/shard_map/ppermute | solution.py:26
  131.7 2.2 collective-permute-start.8
  133.1 1.2 collective-permute-start.9
  133.2 11.2 %copy-start.11 = (f32[8,128,1]{2,1,0:T(8,128)S(1)}, f32[8,128,1]{2,1,0:T(8,128)}, u32[]{:S(2)}) copy-start(f32[8,128,1]{2,1,0:T(8,128)} %copy-done.10) | copy-start | bytes 12292
  133.2 11.2 %copy-start.14 = (f32[8,128,1]{2,1,0:T(8,128)S(1)}, f32[8,128,1]{2,1,0:T(8,128)}, u32[]{:S(2)}) copy-start(f32[8,128,1]{2,1,0:T(8,128)} %copy-done.13) | copy-start | bytes 12292
  134.3 8.6 %collective-permute-start.10 = (f32[1,130,256]{2,1,0:T(8,128)S(1)}, f32[1,130,256]{2,1,0:T(8,128)S(1)}, u32[]{:S(2)}, u32[]{:S(2)}) collective-permute-start(f32[1,130,256]{2,1,0:T(8,128)S(1)} %get-tuple-element.22), channel_id=1, source_target_pairs={{0,1},{1,2},{2,3},{3,4},{4,5},{5,6},{6,7},{7,0},{8,9},{9,10},{10,1... | collective-permute-start | bytes 399368 | tf_op jit(solution)/shard_map/ppermute | solution.py:25
  135.9 8.4 %collective-permute-start.11 = (f32[1,130,256]{2,1,0:T(8,128)S(1)}, f32[1,130,256]{2,1,0:T(8,128)S(1)}, u32[]{:S(2)}, u32[]{:S(2)}) collective-permute-start(f32[1,130,256]{2,1,0:T(8,128)S(1)} %get-tuple-element.23), channel_id=1, source_target_pairs={{1,0},{2,1},{3,2},{4,3},{5,4},{6,5},{7,6},{0,7},{9,8},{10,9},{11,1... | collective-permute-start | bytes 399368 | tf_op jit(solution)/shard_map/ppermute | solution.py:26
  219.9 12.0 %copy-start = (f32[8,128,256]{2,1,0:T(8,128)}, f32[8,128,256]{2,1,0:T(8,128)S(1)}, u32[]{:S(2)}) copy-start(f32[8,128,256]{2,1,0:T(8,128)S(1)} %multiply_add_fusion.1) | copy-start | bytes 3145732
  219.9 1.6 collective-permute-start.12
  220.7 1.2 collective-permute-start.13
  220.8 11.0 %copy-start.12 = (f32[8,128,1]{2,1,0:T(8,128)S(1)}, f32[8,128,1]{2,1,0:T(8,128)}, u32[]{:S(2)}) copy-start(f32[8,128,1]{2,1,0:T(8,128)} %copy-done.10) | copy-start | bytes 12292
  220.8 11.0 %copy-start.15 = (f32[8,128,1]{2,1,0:T(8,128)S(1)}, f32[8,128,1]{2,1,0:T(8,128)}, u32[]{:S(2)}) copy-start(f32[8,128,1]{2,1,0:T(8,128)} %copy-done.13) | copy-start | bytes 12292
  221.9 8.6 %collective-permute-start.14 = (f32[1,130,256]{2,1,0:T(8,128)S(1)}, f32[1,130,256]{2,1,0:T(8,128)S(1)}, u32[]{:S(2)}, u32[]{:S(2)}) collective-permute-start(f32[1,130,256]{2,1,0:T(8,128)S(1)} %get-tuple-element.20), channel_id=1, source_target_pairs={{0,1},{1,2},{2,3},{3,4},{4,5},{5,6},{6,7},{7,0},{8,9},{9,10},{10,1... | collective-permute-start | bytes 399368 | tf_op jit(solution)/shard_map/ppermute | solution.py:25
  223.4 8.4 %collective-permute-start.15 = (f32[1,130,256]{2,1,0:T(8,128)S(1)}, f32[1,130,256]{2,1,0:T(8,128)S(1)}, u32[]{:S(2)}, u32[]{:S(2)}) collective-permute-start(f32[1,130,256]{2,1,0:T(8,128)S(1)} %get-tuple-element.21), channel_id=1, source_target_pairs={{1,0},{2,1},{3,2},{4,3},{5,4},{6,5},{7,6},{0,7},{9,8},{10,9},{11,1... | collective-permute-start | bytes 399368 | tf_op jit(solution)/shard_map/ppermute | solution.py:26
  (7 other events, 67.0 us)
Sparse Core Ops, SparseCore 0:
  14.3 12.2 reduce-scatter.1
  272.5 8.9 all-gather.1
where the time goes:
time: 292 us; the launch traced here: 291 us
  blocking collectives  157 us (54%)
  other arithmetic  43.8 us (15%)
  waiting for transfers between devices  41.5 us (14%)
  starting transfers between devices  22.7 us (8%)
  between operations  20.8 us (7%)
  local copies, waits for them, and re-layouts  5.4 us (2%)
    psum x5, blocking collectives, reduce_one(): summed = lax.psum(value, ('band', 'gz'))  157 us
    ppermute x8, waiting for transfers between devices, extended(): before = lax.ppermute(last, axis, up)  16.2 us
    ppermute x8, starting transfers between devices, extended(): after = lax.ppermute(initial, axis, down)  14.7 us
    reduce_sum x3, other arithmetic, solve(): step_size = inner_now / reduce_one(jnp.sum(direction * image))  14.6 us
    reduce_scatter x1, waiting for transfers between devices, per_device(): lax.psum_scatter(partial_value, 'band', scatter_dimension=1, tiled=True)  12.4 us
    reduce_sum x2, other arithmetic, solve(): inner_next = reduce_one(jnp.sum(residual * precond))  7.89 us
    ppermute x8, starting transfers between devices, extended(): before = lax.ppermute(last, axis, up)  7.82 us
    all_gather x1, waiting for transfers between devices, per_device(): potential = lax.all_gather(solution, 'band', axis=1, tiled=True)  6.76 us
  transfers between devices with their start and end apart: 18, of which 18 were waited for; matrix products, arithmetic and copies ran while one was open for 2% of the time, Pallas kernels for 0%

commit v1 on v0

v1 whole, which is shorter than its diff:
```python
import functools
import math

import jax
import jax.numpy as jnp
from jax import lax
from jax.experimental import pallas as pl
from jax.experimental.pallas import tpu as pltpu
from jax.sharding import PartitionSpec as P

ITERS = 3
ROWS = 32

solvent_eps = 78.36
density_low = 2.0
density_high = 12.0
screening = 0.05
coupling = 1.0 / (4.0 * math.pi)

SINE = (6.2831854820251465, -41.34170150756836, 81.6052474975586, -76.70575714111328, 42.057369232177734, -15.084554672241211, 3.7759575843811035, -0.6150599122047424)


def dielectric(density):
    span = math.log(density_high) - math.log(density_low)
    fraction = jnp.clip((math.log(density_high) - jnp.log(density)) * (1.0 / span), 0.0, 1.0)
    g = fraction - 0.5
    square = g * g
    poly = jnp.full_like(g, SINE[-1])
    for c in SINE[-2::-1]:
        poly = poly * square + c
    turned = 2.0 * math.pi * fraction
    return jnp.exp(math.log(solvent_eps) / (2.0 * math.pi) * (turned + g * poly))


def coefficients(mu, d):
    zero = jnp.zeros_like(mu[0])
    rho = [zero + 1.0]
    direction = [zero + 1.0]
    xi = [zero] * ITERS
    rz = mu[0]
    for step in range(ITERS):
        pap = zero
        for i, a in enumerate(direction):
            for j, b in enumerate(direction):
                pap = pap + a * b * d[i + j]
        alpha = rz / pap
        for i, a in enumerate(direction):
            xi[i] = xi[i] + alpha * a
        image = direction + [zero]
        for i, a in enumerate(direction):
            image[i + 1] = image[i + 1] - a
        rho = rho + [zero]
        rho = [a - alpha * b for a, b in zip(rho, image)]
        if step + 1 < ITERS:
            new = zero
            for i, a in enumerate(rho):
                for j, b in enumerate(rho):
                    new = new + a * b * mu[i + j]
            beta = new / rz
            old = direction + [zero]
            direction = [a + beta * b for a, b in zip(rho, old)]
            rz = new
    return xi, rho


def kernel(gz, orb, bg, occ, core, pot, res, obuf, cbuf, own, sent, got, eps,
           v0, v1, v2, v3, diag, coef, potbuf, resbuf, acc, red,
           in_sem, core_sem, send_sem, recv_sem, rsend, rrecv, out_sem):
    bands, nz, ny, nx = orb.shape
    half_rows = ny // 2
    chunks = half_rows // ROWS
    peers = 2 * gz
    b = lax.axis_index("band")
    z_me = lax.axis_index("gz")
    me = z_me * 2 + b
    base = pl.multiple_of(b * half_rows, half_rows)
    other = pl.multiple_of((1 - b) * half_rows, half_rows)
    partner = {"band": 1 - b}
    up = {"gz": lax.rem(z_me + 1, gz)}
    down = {"gz": lax.rem(z_me + gz - 1, gz)}
    MESH = pl.DeviceIdType.MESH

    def order(i):
        odd = i % 2
        return odd * (nz - 1 - i // 2) + (1 - odd) * (i // 2)

    def plane_in(z):
        return pltpu.make_async_copy(orb.at[:, z], obuf.at[:, z], in_sem.at[z])

    core_in = pltpu.make_async_copy(core.at[:, pl.ds(base, half_rows)], cbuf, core_sem)

    def start_in(i, _):
        plane_in(order(i)).start()
        return 0

    lax.fori_loop(0, nz, start_in, 0)
    core_in.start()

    barrier = pltpu.get_barrier_semaphore()

    def peer_id(j):
        p = lax.rem(me + j, peers)
        return {"gz": p // 2, "band": p % 2}

    def greet(j, _):
        pl.semaphore_signal(barrier, inc=1, device_id=peer_id(j), device_id_type=MESH)
        return 0

    lax.fori_loop(1, peers, greet, 0)
    acc[...] = jnp.zeros_like(acc)
    weights = [occ[bg[k]].astype(jnp.float32) * (1.0 / 1024.0) for k in range(bands)]
    pl.semaphore_wait(barrier, peers - 1)

    def remote(src, dst, s, device):
        return pltpu.make_async_remote_copy(
            src_ref=src, dst_ref=dst, send_sem=send_sem.at[s], recv_sem=recv_sem.at[s],
            device_id=device, device_id_type=MESH)

    def partial_copy(z):
        return remote(sent.at[z], got.at[z], z, partner)

    def squares(z, start, r):
        total = None
        for k in range(bands):
            value = obuf[k, z, pl.ds(start + r * ROWS, ROWS), :].astype(jnp.float32)
            term = weights[k] * (value * value)
            total = term if total is None else total + term
        return total

    def density_plane(i, _):
        z = order(i)
        plane_in(z).wait()

        def theirs(r, _):
            sent[z, pl.ds(r * ROWS, ROWS), :] = squares(z, other, r)
            return 0

        lax.fori_loop(0, chunks, theirs, 0)
        partial_copy(z).start()

        def mine(r, _):
            own[z, pl.ds(r * ROWS, ROWS), :] = squares(z, base, r)
            return 0

        lax.fori_loop(0, chunks, mine, 0)
        return 0

    lax.fori_loop(0, nz, density_plane, 0)
    core_in.wait()

    mine_rows = pl.ds(base, half_rows)

    def edges(buf, s):
        s = nz + 5 * s
        first, last = buf.at[1, mine_rows], buf.at[nz, mine_rows]
        return [
            remote(first, buf.at[nz + 1, mine_rows], s, down),
            remote(last, buf.at[0, mine_rows], s + 1, up),
            remote(first, first, s + 2, partner),
            remote(last, last, s + 3, partner),
        ]

    def inner(buf, s):
        ref = buf.at[pl.ds(2, nz - 2), mine_rows]
        return remote(ref, ref, nz + 5 * s + 4, partner)

    def eps_plane(i, _):
        z = order(i)
        partial_copy(z).wait_recv()

        def chunk(r, _):
            rows = pl.ds(r * ROWS, ROWS)
            electrons = own[z, rows, :] + got[z, rows, :]
            ion = cbuf[z, rows, :]
            own[z, rows, :] = electrons - ion
            eps[z + 1, pl.ds(base + r * ROWS, ROWS), :] = dielectric(electrons + ion)
            return 0

        lax.fori_loop(0, chunks, chunk, 0)
        return 0

    lax.fori_loop(0, 2, eps_plane, 0)
    for c in edges(eps, 0):
        c.start()
    lax.fori_loop(2, nz, eps_plane, 0)
    inner(eps, 0).start()

    row_id = lax.broadcasted_iota(jnp.int32, (ROWS, nx), 0)

    def around(buf, z, r):
        start = pl.multiple_of(base + r * ROWS, ROWS)
        center = buf[z + 1, pl.ds(start, ROWS), :]
        before = buf[z + 1, pl.ds(lax.rem(start + ny - 1, ny), 1), :]
        after = buf[z + 1, pl.ds(lax.rem(start + ROWS, ny), 1), :]
        return center, (
            buf[z, pl.ds(start, ROWS), :],
            buf[z + 2, pl.ds(start, ROWS), :],
            jnp.where(row_id == 0, before, pltpu.roll(center, 1, 0)),
            jnp.where(row_id == ROWS - 1, after, pltpu.roll(center, ROWS - 1, 0)),
            pltpu.roll(center, 1, 1),
            pltpu.roll(center, nx - 1, 1),
        )

    half = 0.5 * coupling

    def coef_chunk(z, r):
        rows = pl.ds(r * ROWS, ROWS)
        center, sides = around(eps, z, r)
        faces = [half * (center + side) for side in sides]
        d = screening + faces[0] + faces[1] + faces[2] + faces[3] + faces[4] + faces[5]
        inverse = 1.0 / d
        diag[z, rows, :] = d
        for f in range(6):
            coef[f, z, rows, :] = faces[f] * inverse
        v0[z + 1, pl.ds(base + r * ROWS, ROWS), :] = own[z, rows, :] * inverse

    def fold(x):
        total = x[0:8]
        for k in range(1, ROWS // 8):
            total = total + x[8 * k:8 * k + 8]
        return total

    def jacobi_chunk(k, src, dst, z, r):
        rows = pl.ds(r * ROWS, ROWS)
        center, sides = around(src, z, r)
        total = coef[0, z, rows, :] * sides[0]
        for f in range(1, 6):
            total = total + coef[f, z, rows, :] * sides[f]
        if k < 2:
            dst[z + 1, pl.ds(base + r * ROWS, ROWS), :] = total
        else:
            dst[z, rows, :] = total
        d = diag[z, rows, :]
        scaled = d * center
        change = d * (center - total)
        acc[2 * k] += fold(center * scaled)
        acc[5 + 2 * k] += fold(center * change)
        if k < 2:
            acc[2 * k + 1] += fold(total * scaled)
            acc[6 + 2 * k] += fold(total * change)

    def stage(s, src, dst, body):
        inner(src, s).wait_recv()

        def one(i, _):
            body(1 + i // chunks, i % chunks)
            return 0

        lax.fori_loop(0, (nz - 2) * chunks, one, 0)
        if dst is not None:
            inner(dst, s + 1).start()
        for c in edges(src, s):
            c.wait_recv()

        def two(i, _):
            body((i // chunks) * (nz - 1), i % chunks)
            return 0

        lax.fori_loop(0, 2 * chunks, two, 0)
        if dst is not None:
            for c in edges(dst, s + 1):
                c.start()

    stage(0, eps, v0, coef_chunk)
    stage(1, v0, v1, functools.partial(jacobi_chunk, 0, v0, v1))
    stage(2, v1, v2, functools.partial(jacobi_chunk, 1, v1, v2))
    stage(3, v2, None, functools.partial(jacobi_chunk, 2, v2, v3))

    row16 = lax.broadcasted_iota(jnp.int32, (16, 128), 0)
    lane16 = lax.broadcasted_iota(jnp.int32, (16, 128), 1)
    sums = jnp.zeros((16, 128), jnp.float32)
    for k in range(10):
        a = acc[k]
        line = jnp.sum(a[:, :128] + a[:, 128:] if nx == 256 else a[:, :128], axis=0, keepdims=True)
        sums = jnp.where(row16 == k, line, sums)
    lanes = jnp.sum(sums, axis=1, keepdims=True)
    red[me] = jnp.sum(jnp.where(row16 == lane16, lanes, 0.0), axis=0, keepdims=True)

    def tell(j):
        return pltpu.make_async_remote_copy(
            src_ref=red.at[me], dst_ref=red.at[me], send_sem=rsend.at[j], recv_sem=rrecv.at[me],
            device_id=peer_id(j), device_id_type=MESH)

    def hear(j):
        p = lax.rem(me + j, peers)
        return pltpu.make_async_remote_copy(
            src_ref=red.at[p], dst_ref=red.at[p], send_sem=rsend.at[j], recv_sem=rrecv.at[p],
            device_id=peer_id(j), device_id_type=MESH)

    def start_tell(j, _):
        tell(j).start()
        return 0

    lax.fori_loop(1, peers, start_tell, 0)

    def wait_hear(j, _):
        hear(j).wait_recv()
        return 0

    lax.fori_loop(1, peers, wait_hear, 0)

    line = jnp.sum(red[...], axis=0)
    totals = jnp.sum(jnp.where(row16 == lane16, line, 0.0), axis=1, keepdims=True)
    wide = jnp.broadcast_to(totals, (16, nx))
    xi, rho = coefficients([wide[k:k + 1] for k in range(5)], [wide[5 + k:6 + k] for k in range(5)])

    def out_copies(z):
        return (
            pltpu.make_async_copy(potbuf.at[z], pot.at[z], out_sem.at[z]),
            pltpu.make_async_copy(resbuf.at[z], res.at[z], out_sem.at[nz + z]),
        )

    def finish(z, _):
        def mine(r, _):
            rows = pl.ds(r * ROWS, ROWS)
            at = pl.ds(base + r * ROWS, ROWS)
            a, c, e = v0[z + 1, at, :], v1[z + 1, at, :], v2[z + 1, at, :]
            potbuf[z, at, :] = xi[0] * a + xi[1] * c + xi[2] * e
            resbuf[z, rows, :] = diag[z, rows, :] * (
                rho[0] * a + rho[1] * c + rho[2] * e + rho[3] * v3[z, rows, :])
            return 0

        def theirs(r, _):
            at = pl.ds(other + r * ROWS, ROWS)
            potbuf[z, at, :] = xi[0] * v0[z + 1, at, :] + xi[1] * v1[z + 1, at, :] + xi[2] * v2[z + 1, at, :]
            return 0

        lax.fori_loop(0, chunks, mine, 0)
        lax.fori_loop(0, chunks, theirs, 0)
        for c in out_copies(z):
            c.start()
        return 0

    lax.fori_loop(0, nz, finish, 0)

    def drain(z, _):
        partial_copy(z).wait_send()
        for c in out_copies(z):
            c.wait()
        return 0

    lax.fori_loop(0, nz, drain, 0)
    for s, buf in enumerate((eps, v0, v1, v2)):
        for c in edges(buf, s):
            c.wait_send()
        inner(buf, s).wait_send()

    def told(j, _):
        tell(j).wait_send()
        return 0

    lax.fori_loop(1, peers, told, 0)


def per_device(gz, orbitals, band_group, occ_table, core_density):
    bands, nz, ny, nx = orbitals.shape
    h = ny // 2
    f32 = jnp.float32
    full = pltpu.VMEM((nz + 2, ny, nx), f32)
    tile = pltpu.VMEM((nz, h, nx), f32)
    copies = nz + 20
    return pl.pallas_call(
        functools.partial(kernel, gz),
        out_shape=(
            jax.ShapeDtypeStruct((nz, ny, nx), f32),
            jax.ShapeDtypeStruct((nz, h, nx), f32),
        ),
        in_specs=[
            pl.BlockSpec(memory_space=pl.ANY),
            pl.BlockSpec(memory_space=pltpu.SMEM),
            pl.BlockSpec(memory_space=pltpu.SMEM),
            pl.BlockSpec(memory_space=pl.ANY),
        ],
        out_specs=(pl.BlockSpec(memory_space=pl.ANY), pl.BlockSpec(memory_space=pl.ANY)),
        scratch_shapes=[
            pltpu.VMEM((bands, nz, ny, nx), jnp.bfloat16),
            tile, tile, tile, tile,
            full, full, full, full,
            tile, tile,
            pltpu.VMEM((6, nz, h, nx), f32),
            pltpu.VMEM((nz, ny, nx), f32),
            tile,
            pltpu.VMEM((10, 8, nx), f32),
            pltpu.VMEM((2 * gz, 1, 128), f32),
            pltpu.SemaphoreType.DMA((nz,)),
            pltpu.SemaphoreType.DMA,
            pltpu.SemaphoreType.DMA((copies,)),
            pltpu.SemaphoreType.DMA((copies,)),
            pltpu.SemaphoreType.DMA((2 * gz,)),
            pltpu.SemaphoreType.DMA((2 * gz,)),
            pltpu.SemaphoreType.DMA((2 * nz,)),
        ],
        compiler_params=pltpu.CompilerParams(
            collective_id=0, has_side_effects=True, vmem_limit_bytes=50 * 1024 * 1024
        ),
        cost_estimate=pl.CostEstimate(flops=30000000, bytes_accessed=12000000, transcendentals=1000000),
        name="poisson",
    )(orbitals, band_group, occ_table, core_density)


def solution(mesh):
    assert mesh.shape["band"] == 2
    return jax.shard_map(
        functools.partial(per_device, mesh.shape["gz"]),
        mesh=mesh,
        in_specs=(
            P(("groups", "band"), "gz", None, None),
            P(("groups", "band")),
            P(),
            P(("groups", "gz"), None, None),
        ),
        out_specs=(P(("groups", "gz"), None, None), P(("groups", "gz"), "band", None)),
        check_vma=False,
    )
```

time: 292 us -> 52.9 us (0.18)
  blocking collectives: 157 us -> 0 us
  Pallas kernels: 0 us -> 48.5 us
  other arithmetic: 43.8 us -> 0 us
  waiting for transfers between devices: 41.5 us -> 0 us
  starting transfers between devices: 22.7 us -> 0 us
  between operations: 20.8 us -> 0.65 us
    psum x5 -> x0, blocking collectives: 157 us -> none  [reduce_one(): summed = lax.psum(value, ('band', 'gz'))]
    pallas_call x0 -> x1, Pallas kernels: none -> 48.5 us  [per_device(): pl.pallas_call(functools.partial(kernel, gz), out_shape=(jax.ShapeDtypeSt...]
    reduce_sum x7 -> x0, other arithmetic: 29.3 us -> none  [the longest x3 14.6 us: solve(): step_size = inner_now / reduce_one(jnp.sum(direction * image))]
    ppermute x16 -> x0, starting transfers between devices: 22.6 us -> none  [the longest x8 14.7 us: extended(): after = lax.ppermute(initial, axis, down)]
    ppermute x16 -> x0, waiting for transfers between devices: 22.4 us -> none  [the longest x8 16.2 us: extended(): before = lax.ppermute(last, axis, up)]
    reduce_scatter x1 -> x0, waiting for transfers between devices: 12.4 us -> none  [per_device(): lax.psum_scatter(partial_value, 'band', scatter_dimension=1, tiled=True)]
    all_gather x1 -> x0, waiting for transfers between devices: 6.76 us -> none  [per_device(): potential = lax.all_gather(solution, 'band', axis=1, tiled=True)]
    add x3 -> x0, other arithmetic: 5.22 us -> none  [the longest x2 2.73 us: solve(): direction = precond + inner_next / inner_now * direction]
  transfers between devices with their start and end apart: 18 -> 0, of which waited for: 18 -> 0; matrix products, arithmetic and copies ran while one was open for 2% -> 0% of each run, Pallas kernels for 0% -> 0%
where the time goes in v1:
time: 52.9 us; the launch traced here: 52.7 us
  Pallas kernels  48.5 us (92%)
  local copies, waits for them, and re-layouts  3.59 us (7%)
  between operations  0.65 us (1%)
    pallas_call x1, Pallas kernels, per_device(): pl.pallas_call(functools.partial(kernel, gz), out_shape=(jax.ShapeDtypeSt...  48.5 us
    unnamed x6, local copies, waits for them, and re-layouts  3.59 us

profile of v1, /device:TPU:0, one launch (start us, length us, event | category | flops | bytes accessed | tf_op | source)
XLA Modules:
  0.0 52.7 jit_solution(8378279276030598920)
XLA Ops:
  0.6 0.0 copy-start
  0.6 0.6 %copy-done = s32[6]{0:T(128)S(1)} copy-done((s32[6]{0:T(128)S(1)}, s32[6]{0:T(128)}, u32[]{:S(2)}) %copy-start) | copy-done | bytes 48
  1.3 0.0 copy-start.1
  1.3 0.7 %copy-done.1 = s32[8]{0:T(128)S(1)} copy-done((s32[8]{0:T(128)S(1)}, s32[8]{0:T(128)}, u32[]{:S(2)}) %copy-start.1) | copy-done | bytes 56
  1.9 48.5 %poisson.1 = (f32[8,256,256]{2,1,0:T(8,128)S(1)}, f32[8,128,256]{2,1,0:T(8,128)S(1)}) custom-call(bf16[6,8,256,256]{3,2,1,0:T(8,128)(2,1)} %orb.1, s32[6]{0:T(128)S(1)} %copy-done, s32[8]{0:T(128)S(1)} %copy-done.1, f32[8,256,256]{2,1,0:T(8,128)} %core.1), custom_call_target="tpu_custom_call" | custom-call | flops 30000000 | bytes 12000000 | tf_op jit(solution)/shard_map/poisson/pallas_call | solution.py:362
  50.4 1.3 %copy.8 = f32[8,256,256]{2,1,0:T(8,128)} copy(f32[8,256,256]{2,1,0:T(8,128)S(1)} %get-tuple-element.4) | data formatting | bytes 4194304
  51.8 1.0 %copy.9 = f32[8,128,256]{2,1,0:T(8,128)} copy(f32[8,128,256]{2,1,0:T(8,128)S(1)} %get-tuple-element.5) | data formatting | bytes 2097152
Async XLA Ops:
  0.6 0.7 %copy-start = (s32[6]{0:T(128)S(1)}, s32[6]{0:T(128)}, u32[]{:S(2)}) copy-start(s32[6]{0:T(128)} %bg.1) | copy-start | bytes 76
  1.3 0.7 %copy-start.1 = (s32[8]{0:T(128)S(1)}, s32[8]{0:T(128)}, u32[]{:S(2)}) copy-start(s32[8]{0:T(128)} %occ.1) | copy-start | bytes 100

commit v2 on v1

--- a/solution.py
+++ b/solution.py
@@ -63,9 +63,9 @@
     return xi, rho
 
 
-def kernel(gz, orb, bg, occ, core, pot, res, obuf, cbuf, own, sent, got, eps,
-           v0, v1, v2, v3, diag, coef, potbuf, resbuf, acc, red,
-           in_sem, core_sem, send_sem, recv_sem, rsend, rrecv, out_sem):
+def kernel(gz, orb, bg_in, occ_in, core, pot, res, obuf, cbuf, own, sent, got, eps,
+           v0, v1, v2, v3, diag, coef, potbuf, resbuf, ys, yh, acc, red,
+           bg, occ, small_sem, in_sem, core_sem, send_sem, recv_sem, rsend, rrecv, out_sem):
     bands, nz, ny, nx = orb.shape
     half_rows = ny // 2
     chunks = half_rows // ROWS
@@ -93,6 +93,12 @@
         plane_in(order(i)).start()
         return 0
 
+    small_in = (
+        pltpu.make_async_copy(bg_in, bg, small_sem.at[0]),
+        pltpu.make_async_copy(occ_in, occ, small_sem.at[1]),
+    )
+    for c in small_in:
+        c.start()
     lax.fori_loop(0, nz, start_in, 0)
     core_in.start()
 
@@ -108,6 +114,8 @@
 
     lax.fori_loop(1, peers, greet, 0)
     acc[...] = jnp.zeros_like(acc)
+    for c in small_in:
+        c.wait()
     weights = [occ[bg[k]].astype(jnp.float32) * (1.0 / 1024.0) for k in range(bands)]
     pl.semaphore_wait(barrier, peers - 1)
 
@@ -135,14 +143,14 @@
             sent[z, pl.ds(r * ROWS, ROWS), :] = squares(z, other, r)
             return 0
 
-        lax.fori_loop(0, chunks, theirs, 0)
+        lax.fori_loop(0, chunks, theirs, 0, unroll=4)
         partial_copy(z).start()
 
         def mine(r, _):
             own[z, pl.ds(r * ROWS, ROWS), :] = squares(z, base, r)
             return 0
 
-        lax.fori_loop(0, chunks, mine, 0)
+        lax.fori_loop(0, chunks, mine, 0, unroll=4)
         return 0
 
     lax.fori_loop(0, nz, density_plane, 0)
@@ -150,19 +158,29 @@
 
     mine_rows = pl.ds(base, half_rows)
 
-    def edges(buf, s):
-        s = nz + 5 * s
+    def edges(buf, k):
+        s = nz + 5 * k
         first, last = buf.at[1, mine_rows], buf.at[nz, mine_rows]
         return [
             remote(first, buf.at[nz + 1, mine_rows], s, down),
             remote(last, buf.at[0, mine_rows], s + 1, up),
-            remote(first, first, s + 2, partner),
-            remote(last, last, s + 3, partner),
+            remote(ys.at[k, pl.ds(0, 2)], yh.at[k, pl.ds(0, 2)], s + 2, partner),
+            remote(ys.at[k, pl.ds(2 * nz - 2, 2)], yh.at[k, pl.ds(2 * nz - 2, 2)], s + 3, partner),
         ]
 
-    def inner(buf, s):
-        ref = buf.at[pl.ds(2, nz - 2), mine_rows]
-        return remote(ref, ref, nz + 5 * s + 4, partner)
+    def inner(s):
+        rows = pl.ds(2, 2 * nz - 4)
+        return remote(ys.at[s, rows], yh.at[s, rows], nz + 5 * s + 4, partner)
+
+    def answer(z):
+        ref = potbuf.at[z, mine_rows]
+        return remote(ref, ref, nz + 20 + z, partner)
+
+    def keep_rows(s, z, r, value):
+        if r == 0:
+            ys[s, 2 * z] = value[:1]
+        if r == chunks - 1:
+            ys[s, 2 * z + 1] = value[ROWS - 1:]
 
     def eps_plane(i, _):
         z = order(i)
@@ -173,25 +191,27 @@
             electrons = own[z, rows, :] + got[z, rows, :]
             ion = cbuf[z, rows, :]
             own[z, rows, :] = electrons - ion
-            eps[z + 1, pl.ds(base + r * ROWS, ROWS), :] = dielectric(electrons + ion)
-            return 0
-
-        lax.fori_loop(0, chunks, chunk, 0)
+            value = dielectric(electrons + ion)
+            eps[z + 1, pl.ds(base + r * ROWS, ROWS), :] = value
+            keep_rows(0, z, r, value)
+
+        for r in range(chunks):
+            chunk(r, 0)
         return 0
 
     lax.fori_loop(0, 2, eps_plane, 0)
     for c in edges(eps, 0):
         c.start()
     lax.fori_loop(2, nz, eps_plane, 0)
-    inner(eps, 0).start()
+    inner(0).start()
 
     row_id = lax.broadcasted_iota(jnp.int32, (ROWS, nx), 0)
 
-    def around(buf, z, r):
+    def around(buf, s, z, r):
         start = pl.multiple_of(base + r * ROWS, ROWS)
         center = buf[z + 1, pl.ds(start, ROWS), :]
-        before = buf[z + 1, pl.ds(lax.rem(start + ny - 1, ny), 1), :]
-        after = buf[z + 1, pl.ds(lax.rem(start + ROWS, ny), 1), :]
+        before = buf[z + 1, pl.ds(start - 1, 1), :] if r > 0 else yh[s, 2 * z + 1]
+        after = buf[z + 1, pl.ds(start + ROWS, 1), :] if r < chunks - 1 else yh[s, 2 * z]
         return center, (
             buf[z, pl.ds(start, ROWS), :],
             buf[z + 2, pl.ds(start, ROWS), :],
@@ -205,14 +225,16 @@
 
     def coef_chunk(z, r):
         rows = pl.ds(r * ROWS, ROWS)
-        center, sides = around(eps, z, r)
+        center, sides = around(eps, 0, z, r)
         faces = [half * (center + side) for side in sides]
         d = screening + faces[0] + faces[1] + faces[2] + faces[3] + faces[4] + faces[5]
         inverse = 1.0 / d
         diag[z, rows, :] = d
         for f in range(6):
             coef[f, z, rows, :] = faces[f] * inverse
-        v0[z + 1, pl.ds(base + r * ROWS, ROWS), :] = own[z, rows, :] * inverse
+        value = own[z, rows, :] * inverse
+        v0[z + 1, pl.ds(base + r * ROWS, ROWS), :] = value
+        keep_rows(1, z, r, value)
 
     def fold(x):
         total = x[0:8]
@@ -222,41 +244,48 @@
 
     def jacobi_chunk(k, src, dst, z, r):
         rows = pl.ds(r * ROWS, ROWS)
-        center, sides = around(src, z, r)
+        center, sides = around(src, k + 1, z, r)
         total = coef[0, z, rows, :] * sides[0]
         for f in range(1, 6):
             total = total + coef[f, z, rows, :] * sides[f]
         if k < 2:
             dst[z + 1, pl.ds(base + r * ROWS, ROWS), :] = total
+            keep_rows(k + 2, z, r, total)
         else:
             dst[z, rows, :] = total
         d = diag[z, rows, :]
         scaled = d * center
         change = d * (center - total)
-        acc[2 * k] += fold(center * scaled)
-        acc[5 + 2 * k] += fold(center * change)
+        sums = [fold(center * scaled), fold(center * change)]
         if k < 2:
-            acc[2 * k + 1] += fold(total * scaled)
-            acc[6 + 2 * k] += fold(total * change)
+            sums += [fold(total * scaled), fold(total * change)]
+        return sums
 
     def stage(s, src, dst, body):
-        inner(src, s).wait_recv()
-
-        def one(i, _):
-            body(1 + i // chunks, i % chunks)
+        k0 = 4 * (s - 1)
+        inner(s).wait_recv()
+
+        def plane(z):
+            sums = [body(z, r) for r in range(chunks)]
+            if sums[0] is not None:
+                for k, parts in enumerate(zip(*sums)):
+                    acc[k0 + k] += sum(parts[1:], parts[0])
+
+        def one(z, _):
+            plane(z)
             return 0
 
-        lax.fori_loop(0, (nz - 2) * chunks, one, 0)
+        lax.fori_loop(1, nz - 1, one, 0)
         if dst is not None:
-            inner(dst, s + 1).start()
+            inner(s + 1).start()
         for c in edges(src, s):
             c.wait_recv()
 
         def two(i, _):
-            body((i // chunks) * (nz - 1), i % chunks)
+            plane(i * (nz - 1))
             return 0
 
-        lax.fori_loop(0, 2 * chunks, two, 0)
+        lax.fori_loop(0, 2, two, 0)
         if dst is not None:
             for c in edges(dst, s + 1):
                 c.start()
@@ -302,7 +331,7 @@
     line = jnp.sum(red[...], axis=0)
     totals = jnp.sum(jnp.where(row16 == lane16, line, 0.0), axis=1, keepdims=True)
     wide = jnp.broadcast_to(totals, (16, nx))
-    xi, rho = coefficients([wide[k:k + 1] for k in range(5)], [wide[5 + k:6 + k] for k in range(5)])
+    xi, rho = coefficients([wide[k:k + 1] for k in range(0, 10, 2)], [wide[k:k + 1] for k in range(1, 10, 2)])
 
     def out_copies(z):
         return (
@@ -310,31 +339,35 @@
             pltpu.make_async_copy(resbuf.at[z], res.at[z], out_sem.at[nz + z]),
         )
 
-    def finish(z, _):
-        def mine(r, _):
+    def potential_plane(z, _):
+        for r in range(chunks):
+            at = pl.ds(base + r * ROWS, ROWS)
+            potbuf[z, at, :] = xi[0] * v0[z + 1, at, :] + xi[1] * v1[z + 1, at, :] + xi[2] * v2[z + 1, at, :]
+        answer(z).start()
+        return 0
+
+    def residual_plane(z, _):
+        for r in range(chunks):
             rows = pl.ds(r * ROWS, ROWS)
             at = pl.ds(base + r * ROWS, ROWS)
-            a, c, e = v0[z + 1, at, :], v1[z + 1, at, :], v2[z + 1, at, :]
-            potbuf[z, at, :] = xi[0] * a + xi[1] * c + xi[2] * e
             resbuf[z, rows, :] = diag[z, rows, :] * (
-                rho[0] * a + rho[1] * c + rho[2] * e + rho[3] * v3[z, rows, :])
-            return 0
-
-        def theirs(r, _):
-            at = pl.ds(other + r * ROWS, ROWS)
-            potbuf[z, at, :] = xi[0] * v0[z + 1, at, :] + xi[1] * v1[z + 1, at, :] + xi[2] * v2[z + 1, at, :]
-            return 0
-
-        lax.fori_loop(0, chunks, mine, 0)
-        lax.fori_loop(0, chunks, theirs, 0)
-        for c in out_copies(z):
-            c.start()
-        return 0
-
-    lax.fori_loop(0, nz, finish, 0)
+                rho[0] * v0[z + 1, at, :] + rho[1] * v1[z + 1, at, :]
+                + rho[2] * v2[z + 1, at, :] + rho[3] * v3[z, rows, :])
+        out_copies(z)[1].start()
+        return 0
+
+    def potential_out(z, _):
+        answer(z).wait_recv()
+        out_copies(z)[0].start()
+        return 0
+
+    lax.fori_loop(0, nz, potential_plane, 0)
+    lax.fori_loop(0, nz, residual_plane, 0)
+    lax.fori_loop(0, nz, potential_out, 0)
 
     def drain(z, _):
         partial_copy(z).wait_send()
+        answer(z).wait_send()
         for c in out_copies(z):
             c.wait()
         return 0
@@ -343,7 +376,7 @@
     for s, buf in enumerate((eps, v0, v1, v2)):
         for c in edges(buf, s):
             c.wait_send()
-        inner(buf, s).wait_send()
+        inner(s).wait_send()
 
     def told(j, _):
         tell(j).wait_send()
@@ -358,7 +391,7 @@
     f32 = jnp.float32
     full = pltpu.VMEM((nz + 2, ny, nx), f32)
     tile = pltpu.VMEM((nz, h, nx), f32)
-    copies = nz + 20
+    copies = 2 * nz + 20
     return pl.pallas_call(
         functools.partial(kernel, gz),
         out_shape=(
@@ -366,10 +399,10 @@
             jax.ShapeDtypeStruct((nz, h, nx), f32),
         ),
         in_specs=[
-            pl.BlockSpec(memory_space=pl.ANY),
-            pl.BlockSpec(memory_space=pltpu.SMEM),
-            pl.BlockSpec(memory_space=pltpu.SMEM),
-            pl.BlockSpec(memory_space=pl.ANY),
+            pl.BlockSpec(memory_space=pltpu.HBM),
+            pl.BlockSpec(memory_space=pltpu.HBM),
+            pl.BlockSpec(memory_space=pltpu.HBM),
+            pl.BlockSpec(memory_space=pltpu.HBM),
         ],
         out_specs=(pl.BlockSpec(memory_space=pl.ANY), pl.BlockSpec(memory_space=pl.ANY)),
         scratch_shapes=[
@@ -380,8 +413,13 @@
             pltpu.VMEM((6, nz, h, nx), f32),
             pltpu.VMEM((nz, ny, nx), f32),
             tile,
+            pltpu.VMEM((4, 2 * nz, 1, nx), f32),
+            pltpu.VMEM((4, 2 * nz, 1, nx), f32),
             pltpu.VMEM((10, 8, nx), f32),
             pltpu.VMEM((2 * gz, 1, 128), f32),
+            pltpu.SMEM(band_group.shape, jnp.int32),
+            pltpu.SMEM(occ_table.shape, jnp.int32),
+            pltpu.SemaphoreType.DMA((2,)),
             pltpu.SemaphoreType.DMA((nz,)),
             pltpu.SemaphoreType.DMA,
             pltpu.SemaphoreType.DMA((copies,)),

time: 52.9 us -> 49.2 us (0.930)
  Pallas kernels: 48.5 us -> 44.8 us
    pallas_call x1, Pallas kernels: 48.5 us -> 44.8 us  [per_device(): pl.pallas_call(functools.partial(kernel, gz), out_shape=(jax.ShapeDtypeSt...]
where the time goes in v2:
time: 49.2 us; the launch traced here: 49.1 us
  Pallas kernels  44.8 us (91%)
  local copies, waits for them, and re-layouts  3.59 us (7%)
  between operations  0.65 us (1%)
    pallas_call x1, Pallas kernels, per_device(): pl.pallas_call(functools.partial(kernel, gz), out_shape=(jax.ShapeDtypeSt...  44.8 us
    unnamed x6, local copies, waits for them, and re-layouts  3.59 us

profile of v2, /device:TPU:0, one launch (start us, length us, event | category | flops | bytes accessed | tf_op | source)
XLA Modules:
  0.0 49.1 jit_solution(11960269999905101076)
XLA Ops:
  0.6 0.0 copy-start
  0.6 0.6 %copy-done = s32[6]{0:T(128)S(1)} copy-done((s32[6]{0:T(128)S(1)}, s32[6]{0:T(128)}, u32[]{:S(2)}) %copy-start) | copy-done | bytes 48
  1.3 0.0 copy-start.1
  1.3 0.7 %copy-done.1 = s32[8]{0:T(128)S(1)} copy-done((s32[8]{0:T(128)S(1)}, s32[8]{0:T(128)}, u32[]{:S(2)}) %copy-start.1) | copy-done | bytes 56
  1.9 44.8 %poisson.1 = (f32[8,256,256]{2,1,0:T(8,128)S(1)}, f32[8,128,256]{2,1,0:T(8,128)S(1)}) custom-call(bf16[6,8,256,256]{3,2,1,0:T(8,128)(2,1)} %orb.1, s32[6]{0:T(128)S(1)} %copy-done, s32[8]{0:T(128)S(1)} %copy-done.1, f32[8,256,256]{2,1,0:T(8,128)} %core.1), custom_call_target="tpu_custom_call" | custom-call | flops 30000000 | bytes 12000000 | tf_op jit(solution)/shard_map/poisson/pallas_call | solution.py:395
  46.8 1.3 %copy.8 = f32[8,256,256]{2,1,0:T(8,128)} copy(f32[8,256,256]{2,1,0:T(8,128)S(1)} %get-tuple-element.4) | data formatting | bytes 4194304
  48.1 1.0 %copy.9 = f32[8,128,256]{2,1,0:T(8,128)} copy(f32[8,128,256]{2,1,0:T(8,128)S(1)} %get-tuple-element.5) | data formatting | bytes 2097152
Async XLA Ops:
  0.6 0.7 %copy-start = (s32[6]{0:T(128)S(1)}, s32[6]{0:T(128)}, u32[]{:S(2)}) copy-start(s32[6]{0:T(128)} %bg_in.1) | copy-start | bytes 76
  1.3 0.7 %copy-start.1 = (s32[8]{0:T(128)S(1)}, s32[8]{0:T(128)}, u32[]{:S(2)}) copy-start(s32[8]{0:T(128)} %occ_in.1) | copy-start | bytes 100
